TPU v7x, 32 devices: a whole 2x2x4 slice. The times are simulated.
32 devices in a mesh: tm: 4 (over z), ha: 2 (over y), wa: 4 (over x, core).
Axes of the slice: x: 2, y: 2, z: 4, core: 2. Of those that a mesh axis runs over, the one named last changes fastest.
Arguments:
- latent: bfloat16 [8, 32, 64, 512], P('tm', 'ha', 'wa'), may hold values from -1300 to 1300
- norm_gain: float32 [512], replicated, may hold values from 0.1 to 1.9
- norm_bias: float32 [512], replicated, may hold values from -3 to 3
- conv_weight: bfloat16 [3, 3, 3, 512, 256], replicated, may hold values from -0.0546875 to 0.0546875
- conv_bias: float32 [256], replicated, may hold values from -3 to 3
- up_weight: bfloat16 [4, 4, 256, 256], replicated, may hold values from -0.1875 to 0.1875
- up_bias: float32 [256], replicated, may hold values from -3 to 3
Outputs:
- video: bfloat16 [8, 64, 128, 256], P('tm', 'ha', 'wa')
All inputs are finite; a program needn't handle non-finite values.
Results may differ from a plain program's by a relative error of at most 0.0054.
Values may be sent and summed in bfloat16 or wider, within the bound.
A program may use at most 64 MiB of HBM per device.

v0:
```python
import jax
import jax.numpy as jnp
from jax import lax
from jax.sharding import PartitionSpec as P

GROUPS = 32


def prefix(part, axis, combine, identity):
    place = lax.axis_index(axis)
    gathered = jax.tree.map(lambda a: lax.all_gather(a, axis), part)
    state = jax.tree.map(lambda a, e: jnp.zeros_like(a) + jnp.asarray(e, a.dtype), part, identity)

    def one(hop, state):
        return combine(
            state, jax.tree.map(lambda a: lax.dynamic_index_in_dim(a, hop, 0, False), gathered)
        )

    return lax.fori_loop(0, place, one, state)


def padded_2(block, sides, width):
    for axis, dim in sides:
        count = lax.axis_size(axis)
        forward = [(i, i + 1) for i in range(count - 1)]
        backward = [(target, source) for source, target in forward]
        low = lax.ppermute(
            lax.slice_in_dim(block, block.shape[dim] - width, None, axis=dim), axis, forward
        )
        high = lax.ppermute(lax.slice_in_dim(block, 0, width, axis=dim), axis, backward)
        block = jnp.concatenate([low, block, high], axis=dim)
    return block


def from_behind(array, axis, by):
    devices = lax.axis_size(axis)
    pairs = [(i, i + by) for i in range(devices) if 0 <= i + by < devices]
    return lax.ppermute(array, axis, pairs)


def group_totals(latent):
    wide = latent.astype(jnp.float32)
    sums = jnp.sum(wide, axis=(0, 1, 2)).reshape(GROUPS, -1).sum(axis=1)
    squares = jnp.sum(wide * wide, axis=(0, 1, 2)).reshape(GROUPS, -1).sum(axis=1)
    return (sums, squares)


def add_pair(earlier, later):
    return (earlier[0] + later[0], earlier[1] + later[1])


def tap_sum(source, weights, height, breadth):
    count = source.shape[0]
    summed = None
    for row_tap in range(3):
        joined = jnp.concatenate(
            [
                source[:, row_tap : row_tap + height, col_tap : col_tap + breadth, :]
                for col_tap in range(3)
            ],
            axis=-1,
        )
        joined = joined.reshape(count * height * breadth, -1)
        term = jnp.dot(
            joined,
            weights[row_tap].reshape(-1, weights.shape[-1]),
            preferred_element_type=jnp.float32,
        )
        summed = term if summed is None else summed + term
    return summed


def upsample_tile(values, up_weight):
    frames, height, breadth, chans = values.shape
    flat = values.reshape(frames * height * breadth, chans)
    rows_out = []
    for row_par in (0, 1):
        cols_out = []
        for col_par in (0, 1):
            joined = jnp.concatenate(
                [
                    up_weight[row_par + 2 * shift_row, col_par + 2 * shift_col]
                    for shift_row in (0, 1)
                    for shift_col in (0, 1)
                ],
                axis=1,
            )
            product = jnp.dot(flat, joined, preferred_element_type=jnp.float32).reshape(
                frames, height, breadth, 4, chans
            )
            summed = jnp.zeros((frames, height + 1, breadth + 1, chans), jnp.float32)
            for shift_row in (0, 1):
                for shift_col in (0, 1):
                    summed = summed + jnp.pad(
                        product[:, :, :, 2 * shift_row + shift_col],
                        ((0, 0), (shift_row, 1 - shift_row), (shift_col, 1 - shift_col), (0, 0)),
                    )
            cols_out.append(summed)
        rows_out.append(jnp.stack(cols_out, axis=3))
    return jnp.stack(rows_out, axis=2).reshape(frames, 2 * height + 2, 2 * breadth + 2, chans)


def shards(latent, norm_gain, norm_bias, conv_weight, conv_bias, up_weight, up_bias):
    frames, height, breadth, channels = latent.shape
    block_index = lax.axis_index("tm")
    tile_sums, tile_squares = group_totals(latent)
    block_sums, block_squares = lax.psum((tile_sums, tile_squares), ("ha", "wa"))
    zeros_pair = (jnp.zeros_like(block_sums), jnp.zeros_like(block_squares))
    before = prefix((block_sums, block_squares), "tm", add_pair, zeros_pair)
    upto_sums = before[0] + block_sums
    upto_squares = before[1] + block_squares
    group_width = channels // GROUPS
    cells = float(
        frames * height * breadth * lax.axis_size("ha") * lax.axis_size("wa") * group_width
    )
    counted = (block_index + 1).astype(jnp.float32) * cells
    mean = upto_sums / counted
    variance = upto_squares / counted - mean * mean
    inverse = lax.rsqrt(variance + 1e-06)
    mean_chan = jnp.repeat(mean, group_width)
    inverse_chan = jnp.repeat(inverse, group_width)
    normed = jax.nn.silu(
        (latent.astype(jnp.float32) - mean_chan) * inverse_chan * norm_gain + norm_bias
    ).astype(jnp.bfloat16)
    padded = padded_2(normed, (("ha", 1), ("wa", 2)), 1)
    earlier = from_behind(padded, "tm", 1)
    opening = jnp.stack([padded[0], padded[0]])
    earlier = jnp.where(block_index == 0, opening, earlier)
    extended = jnp.concatenate([earlier, padded], axis=0)
    summed = None
    for lag_step in range(3):
        term = tap_sum(
            extended[lag_step : lag_step + frames], conv_weight[lag_step], height, breadth
        )
        summed = term if summed is None else summed + term
    features = (summed + conv_bias).astype(jnp.bfloat16).reshape(frames, height, breadth, -1)
    spread = upsample_tile(features, up_weight)
    from_above = from_behind(spread[:, -1].astype(jnp.bfloat16), "ha", 1).astype(jnp.float32)
    from_below = from_behind(spread[:, 0].astype(jnp.bfloat16), "ha", -1).astype(jnp.float32)
    middle = spread[:, 1:-1]
    middle = middle.at[:, 0].add(from_above)
    middle = middle.at[:, -1].add(from_below)
    from_left = from_behind(middle[:, :, -1].astype(jnp.bfloat16), "wa", 1).astype(jnp.float32)
    from_right = from_behind(middle[:, :, 0].astype(jnp.bfloat16), "wa", -1).astype(jnp.float32)
    inner = middle[:, :, 1:-1]
    inner = inner.at[:, :, 0].add(from_left)
    inner = inner.at[:, :, -1].add(from_right)
    return (inner + up_bias).astype(jnp.bfloat16)


def solution(mesh):
    in_specs = (P("tm", "ha", "wa", None), P(), P(), P(), P(), P(), P())
    out_specs = P("tm", "ha", "wa", None)
    return jax.shard_map(shards, mesh=mesh, in_specs=in_specs, out_specs=out_specs, check_vma=False)
```

profile of v0, /device:TPU:9, one launch (start us, length us, event | category | flops | bytes accessed | tf_op | source)
XLA Modules:
  0.0 143.2 jit_solution(13787219909280827165)
XLA Ops:
  0.0 1.2 fusion.9
  1.6 11.8 %all-reduce.18 = (f32[32]{0:T(128)S(1)}, f32[32]{0:T(128)S(1)}) all-reduce(f32[32]{0:T(128)S(1)} %reduce_sum.37, f32[32]{0:T(128)S(1)} %reduce_sum.39), channel_id=1, replica_groups=mesh['tm'=4,'ha'=2,'wa'=4] {'ha','wa'}, use_global_device_ids=true, to_apply=%region_2.0 | all-reduce | flops 64 | bytes 512 | tf_op jit(solution)/shard_map/psum | solution.py:107
  13.4 1.2 dynamic-slice.32
  15.7 6.9 %all-reduce.19 = (f32[128]{0:T(128)S(1)}, f32[128]{0:T(128)S(1)}) all-reduce(f32[128]{0:T(128)S(1)} %dynamic-update-slice.12, f32[128]{0:T(128)S(1)} %dynamic-update-slice.13), channel_id=2, replica_groups=mesh['tm'=4,'ha'=2,'wa'=4] {'tm'}, use_global_device_ids=true, to_apply=%add.16 | all-reduce | flops 256 | bytes 2048
  23.1 1.4 %fusion.18 = bf16[2,16,16,512]{3,2,1,0:T(8,128)(2,1)S(1)} fusion(bf16[2,16,16,512]{3,2,1,0:T(8,128)(2,1)} %param.17, f32[512]{0:T(512)} %param.19, f32[512]{0:T(512)} %param.18, f32[512]{0:T(512)S(1)} %mul.34, f32[512]{0:T(512)S(1)} %sub.13), kind=kLoop, calls=%fused_computation.42 | loop fusion | flops 2621440 | bytes 1056768 | tf_op jit(solution)/shard_map/convert_element_type | solution.py:124
  24.6 1.3 collective-permute-start.1
  25.9 4.0 %collective-permute-start = (bf16[2,1,16,512]{3,2,1,0:T(8,128)(2,1)S(1)}, bf16[2,1,16,512]{3,2,1,0:T(8,128)(2,1)S(1)}, u32[]{:S(2)}, u32[]{:S(2)}) collective-permute-start(bf16[2,1,16,512]{3,2,1,0:T(8,128)(2,1)S(1)} %get-tuple-element.187), channel_id=1, source_target_pairs={{0,4},{1,5},{2,6},{3,7},{8,12},{9,13},{10,14},{11,15},{16,20},{17,... | collective-permute-start | bytes 98312 | tf_op jit(solution)/shard_map/ppermute | solution.py:27
  29.9 5.9 %fusion.58 = (bf16[1,1,3,512,256]{4,3,2,1,0:T(8,128)(2,1)S(1)}, bf16[1,1,3,512,256]{4,3,2,1,0:T(8,128)(2,1)}, bf16[1,1,3,512,256]{4,3,2,1,0:T(8,128)(2,1)}, bf16...) fusion(bf16[3,3,3,512,256]{4,3,2,1,0:T(8,128)(2,1)} %param.20), kind=kLoop, calls=%fused_computation.136 | loop fusion | bytes 14155776 | tf_op jit(solution)/shard_map/slice | solution.py:66
  36.0 7.0 %collective-permute-start.3 = (bf16[2,18,1,512]{3,2,1,0:T(2,128)(2,1)S(1)}, bf16[2,18,1,512]{3,2,1,0:T(2,128)(2,1)S(1)}, u32[]{:S(2)}, u32[]{:S(2)}) collective-permute-start(bf16[2,18,1,512]{3,2,1,0:T(2,128)(2,1)S(1)} %get-tuple-element.183), channel_id=1, source_target_pairs={{1,0},{2,1},{3,2},{5,4},{6,5},{7,6},{9,8},{10,9},{11,10},{13,12},{... | collective-permute-start | bytes 110600 | tf_op jit(solution)/shard_map/ppermute | solution.py:30
  43.0 1.9 %collective-permute-start.2 = (bf16[2,18,1,512]{3,2,1,0:T(2,128)(2,1)S(1)}, bf16[2,18,1,512]{3,2,1,0:T(2,128)(2,1)S(1)}, u32[]{:S(2)}, u32[]{:S(2)}) collective-permute-start(bf16[2,18,1,512]{3,2,1,0:T(2,128)(2,1)S(1)} %get-tuple-element.182), channel_id=1, source_target_pairs={{0,1},{1,2},{2,3},{4,5},{5,6},{6,7},{8,9},{9,10},{10,11},{12,13},{... | collective-permute-start | bytes 110600 | tf_op jit(solution)/shard_map/ppermute | solution.py:27
  44.9 1.2 slice_bitcast_fusion.15
  46.8 3.2 %collective-permute-start.4 = (bf16[2,18,18,512]{3,2,1,0:T(8,128)(2,1)S(1)}, bf16[2,18,18,512]{3,2,1,0:T(8,128)(2,1)S(1)}, u32[]{:S(2)}, u32[]{:S(2)}) collective-permute-start(bf16[2,18,18,512]{3,2,1,0:T(8,128)(2,1)S(1)} %pad_maximum_fusion.10), channel_id=1, source_target_pairs={{0,8},{8,16},{16,24},{1,9},{9,17},{17,25},{2,10},{10,18},{18,26},{... | collective-permute-start | bytes 1990664 | tf_op jit(solution)/shard_map/ppermute | solution.py:38
  53.4 17.6 %collective-permute-done.4 = bf16[2,18,18,512]{3,2,1,0:T(8,128)(2,1)S(1)} collective-permute-done((bf16[2,18,18,512]{3,2,1,0:T(8,128)(2,1)S(1)}, bf16[2,18,18,512]{3,2,1,0:T(8,128)(2,1)S(1)}, u32[]{:S(2)}, u32[]{:S(2)}) %collective-permute-start.4) | collective-permute-done | bytes 663584 | tf_op jit(solution)/shard_map/ppermute | solution.py:38
  73.4 0.8 copy-done.1
  75.1 0.8 copy-done
  77.2 1.0 copy-done.6
  79.5 1.0 copy-done.4
  82.2 1.8 %fusion.43 = f32[512,1024]{1,0:T(8,128)} fusion(bf16[512,256]{1,0:T(8,128)(2,1)S(1)} %fusion.8, bf16[256,256]{1,0:T(8,128)(2,1)S(1)} %copy-done.30, bf16[256,256]{1,0:T(8,128)(2,1)S(1)} %copy-done.31, bf16[256,256]{1,0:T(8,128)(2,1)S(1)} %get-tuple-element.125, bf16[256,256]{1,0:T(8,128)(2,1)S(1)} %get-tuple-element.126), kind=kOutput, calls=%fused_computation.75 | convolution fusion | flops 270532608 | bytes 2883584 | tf_op jit(solution)/shard_map/dot_general | solution.py:88
  84.0 2.2 %reshape.235 = f32[2,16,16,4,256]{4,3,2,1,0:T(4,128)S(1)} reshape(f32[512,1024]{1,0:T(8,128)} %fusion.43) | data formatting | bytes 4194304 | tf_op jit(solution)/shard_map/reshape | solution.py:88
  86.2 1.9 %fusion.62 = (f32[2,16,16,1,256]{4,3,2,1,0:T(1,128)S(1)}, f32[2,16,16,1,256]{4,3,2,1,0:T(1,128)S(1)}, f32[2,16,16,1,256]{4,3,2,1,0:T(1,128)S(1)}, f32[2,16,16,1,256]{4,3,2,1,0:T(1,128)S(1)}) fusion(f32[2,16,16,4,256]{4,3,2,1,0:T(4,128)S(1)} %reshape.235), kind=kLoop, calls=%fused_computation.140 | loop fusion | bytes 4194304 | tf_op jit(solution)/shard_map/slice | solution.py:95
  88.2 0.8 copy.82
  89.0 0.8 copy.83
  89.9 1.8 %fusion.35 = f32[512,1024]{1,0:T(8,128)} fusion(bf16[512,256]{1,0:T(8,128)(2,1)S(1)} %fusion.8, bf16[256,256]{1,0:T(8,128)(2,1)S(1)} %copy-done.26, bf16[256,256]{1,0:T(8,128)(2,1)S(1)} %copy-done.27, bf16[256,256]{1,0:T(8,128)(2,1)S(1)} %copy-done.28, bf16[256,256]{1,0:T(8,128)(2,1)S(1)} %copy-done.29), kind=kOutput, calls=%fused_computation.67 | convolution fusion | flops 270532608 | bytes 2883584 | tf_op jit(solution)/shard_map/dot_general | solution.py:88
  91.7 2.2 %reshape.234 = f32[2,16,16,4,256]{4,3,2,1,0:T(4,128)S(1)} reshape(f32[512,1024]{1,0:T(8,128)} %fusion.35) | data formatting | bytes 4194304 | tf_op jit(solution)/shard_map/reshape | solution.py:88
  93.9 1.9 %fusion.61 = (f32[2,16,16,1,256]{4,3,2,1,0:T(1,128)S(1)}, f32[2,16,16,1,256]{4,3,2,1,0:T(1,128)S(1)}, f32[2,16,16,1,256]{4,3,2,1,0:T(1,128)S(1)}, f32[2,16,16,1,256]{4,3,2,1,0:T(1,128)S(1)}) fusion(f32[2,16,16,4,256]{4,3,2,1,0:T(4,128)S(1)} %reshape.234), kind=kLoop, calls=%fused_computation.139 | loop fusion | bytes 4194304 | tf_op jit(solution)/shard_map/slice | solution.py:95
  95.8 0.8 copy.84
  96.7 0.8 copy.85
  97.5 0.8 copy.86
  98.3 0.8 copy.87
  99.2 1.8 %fusion.27 = f32[512,1024]{1,0:T(8,128)} fusion(bf16[512,256]{1,0:T(8,128)(2,1)S(1)} %fusion.8, bf16[256,256]{1,0:T(8,128)(2,1)S(1)} %copy-done.22, bf16[256,256]{1,0:T(8,128)(2,1)S(1)} %copy-done.23, bf16[256,256]{1,0:T(8,128)(2,1)S(1)} %copy-done.24, bf16[256,256]{1,0:T(8,128)(2,1)S(1)} %copy-done.25), kind=kOutput, calls=%fused_computation.59 | convolution fusion | flops 270532608 | bytes 2883584 | tf_op jit(solution)/shard_map/dot_general | solution.py:88
  101.0 2.2 %reshape.233 = f32[2,16,16,4,256]{4,3,2,1,0:T(4,128)S(1)} reshape(f32[512,1024]{1,0:T(8,128)} %fusion.27) | data formatting | bytes 4194304 | tf_op jit(solution)/shard_map/reshape | solution.py:88
  103.2 1.9 %fusion.60 = (f32[2,16,16,1,256]{4,3,2,1,0:T(1,128)S(1)}, f32[2,16,16,1,256]{4,3,2,1,0:T(1,128)S(1)}, f32[2,16,16,1,256]{4,3,2,1,0:T(1,128)S(1)}, f32[2,16,16,1,256]{4,3,2,1,0:T(1,128)S(1)}) fusion(f32[2,16,16,4,256]{4,3,2,1,0:T(4,128)S(1)} %reshape.233), kind=kLoop, calls=%fused_computation.138 | loop fusion | bytes 4194304 | tf_op jit(solution)/shard_map/slice | solution.py:95
  105.1 0.9 copy.88
  106.0 0.9 copy.89
  106.8 0.8 copy.90
  108.9 2.0 %reshape.232 = f32[2,16,16,4,256]{4,3,2,1,0:T(4,128)} reshape(f32[512,1024]{1,0:T(8,128)S(1)} %fusion.19) | data formatting | bytes 4194304 | tf_op jit(solution)/shard_map/reshape | solution.py:88
  111.0 5.9 %fusion.59 = (f32[2,16,16,1,256]{4,3,2,1,0:T(1,128)S(1)}, f32[2,16,16,1,256]{4,3,2,1,0:T(1,128)S(1)}, f32[2,16,16,1,256]{4,3,2,1,0:T(1,128)S(1)}, f32[2,16,16,1,256]{4,3,2,1,0:T(1,128)S(1)}) fusion(f32[2,16,16,4,256]{4,3,2,1,0:T(4,128)} %reshape.232), kind=kLoop, calls=%fused_computation.137 | loop fusion | bytes 4194304 | tf_op jit(solution)/shard_map/slice | solution.py:95
  117.1 0.9 copy-done.9
  119.2 0.9 copy-done.15
  121.6 1.2 copy.43
  123.7 1.3 collective-permute-start.5
  125.8 1.3 collective-permute-start.6
  127.6 2.9 %collective-permute-done.6 = bf16[2,34,256]{2,0,1:T(2,128)(2,1)S(1)} collective-permute-done((bf16[2,34,256]{2,0,1:T(2,128)(2,1)S(1)}, bf16[2,34,256]{2,0,1:T(2,128)(2,1)S(1)}, u32[]{:S(2)}, u32[]{:S(2)}) %collective-permute-start.6) | collective-permute-done | bytes 34848 | tf_op jit(solution)/shard_map/ppermute | solution.py:38
  130.6 2.8 %scatter-add.15 = f32[2,32,34,256]{3,1,0,2:T(8,128)S(1)} dynamic-update-slice(f32[2,32,34,256]{3,1,0,2:T(8,128)S(1)} %copy.45, f32[2,1,34,256]{3,1,0,2:T(1,128)S(1)} %copy_add_fusion, s32[]{:T(128)} %constant.128.clone.1, s32[]{:T(128)} %constant.134.clone.1, s32[]{:T(128)} %constant.128.clone.1, s32[]{:T(128)} %constant.128.clone.1) | dynamic-update-slice | bytes 139268 | tf_op jit(solution)/shard_map/scatter-add | solution.py:142
  133.7 2.2 %collective-permute-start.7 = (bf16[2,32,256]{2,1,0:T(8,128)(2,1)S(1)}, bf16[2,32,256]{2,1,0:T(8,128)(2,1)S(1)}, u32[]{:S(2)}, u32[]{:S(2)}) collective-permute-start(bf16[2,32,256]{2,1,0:T(8,128)(2,1)S(1)} %get-tuple-element.164), channel_id=1, source_target_pairs={{0,1},{1,2},{2,3},{4,5},{5,6},{6,7},{8,9},{9,10},{10,11},{12,13},{... | collective-permute-start | bytes 98312 | tf_op jit(solution)/shard_map/ppermute | solution.py:38
  136.0 3.0 %collective-permute-start.8 = (bf16[2,32,256]{2,1,0:T(8,128)(2,1)S(1)}, bf16[2,32,256]{2,1,0:T(8,128)(2,1)S(1)}, u32[]{:S(2)}, u32[]{:S(2)}) collective-permute-start(bf16[2,32,256]{2,1,0:T(8,128)(2,1)S(1)} %get-tuple-element.163), channel_id=1, source_target_pairs={{1,0},{2,1},{3,2},{5,4},{6,5},{7,6},{9,8},{10,9},{11,10},{13,12},{... | collective-permute-start | bytes 98312 | tf_op jit(solution)/shard_map/ppermute | solution.py:38
  139.1 2.2 %collective-permute-done.8 = bf16[2,32,256]{2,1,0:T(8,128)(2,1)S(1)} collective-permute-done((bf16[2,32,256]{2,1,0:T(8,128)(2,1)S(1)}, bf16[2,32,256]{2,1,0:T(8,128)(2,1)S(1)}, u32[]{:S(2)}, u32[]{:S(2)}) %collective-permute-start.8) | collective-permute-done | bytes 32800 | tf_op jit(solution)/shard_map/ppermute | solution.py:38
  141.6 1.6 %copy.46 = bf16[2,32,32,256]{3,2,1,0:T(8,128)(2,1)} copy(bf16[2,32,32,256]{3,1,0,2:T(8,128)(2,1)S(1)} %add_convert_fusion) | data formatting | bytes 2097152 | tf_op jit(solution)/shard_map/convert_element_type | solution.py:148
  (140 shorter events, 19.9 us)
Async XLA Ops:
  24.6 11.3 %collective-permute-start.1 = (bf16[2,1,16,512]{3,2,1,0:T(8,128)(2,1)S(1)}, bf16[2,1,16,512]{3,2,1,0:T(8,128)(2,1)S(1)}, u32[]{:S(2)}, u32[]{:S(2)}) collective-permute-start(bf16[2,1,16,512]{3,2,1,0:T(8,128)(2,1)S(1)} %get-tuple-element.188), channel_id=1, source_target_pairs={{4,0},{5,1},{6,2},{7,3},{12,8},{13,9},{14,10},{15,11},{20,16},{21,... | collective-permute-start | bytes 98312 | tf_op jit(solution)/shard_map/ppermute | solution.py:30
  25.9 10.0 %collective-permute-start = (bf16[2,1,16,512]{3,2,1,0:T(8,128)(2,1)S(1)}, bf16[2,1,16,512]{3,2,1,0:T(8,128)(2,1)S(1)}, u32[]{:S(2)}, u32[]{:S(2)}) collective-permute-start(bf16[2,1,16,512]{3,2,1,0:T(8,128)(2,1)S(1)} %get-tuple-element.187), channel_id=1, source_target_pairs={{0,4},{1,5},{2,6},{3,7},{8,12},{9,13},{10,14},{11,15},{16,20},{17,... | collective-permute-start | bytes 98312 | tf_op jit(solution)/shard_map/ppermute | solution.py:27
  29.9 15.0 %copy-start.8 = (bf16[4,4,256,256]{3,2,1,0:T(8,128)(2,1)S(1)}, bf16[4,4,256,256]{3,2,1,0:T(8,128)(2,1)}, u32[]{:S(2)}) copy-start(bf16[4,4,256,256]{3,2,1,0:T(8,128)(2,1)} %param.22) | copy-start | bytes 6291460
  36.0 10.2 %collective-permute-start.3 = (bf16[2,18,1,512]{3,2,1,0:T(2,128)(2,1)S(1)}, bf16[2,18,1,512]{3,2,1,0:T(2,128)(2,1)S(1)}, u32[]{:S(2)}, u32[]{:S(2)}) collective-permute-start(bf16[2,18,1,512]{3,2,1,0:T(2,128)(2,1)S(1)} %get-tuple-element.183), channel_id=1, source_target_pairs={{1,0},{2,1},{3,2},{5,4},{6,5},{7,6},{9,8},{10,9},{11,10},{13,12},{... | collective-permute-start | bytes 110600 | tf_op jit(solution)/shard_map/ppermute | solution.py:30
  43.0 3.3 %collective-permute-start.2 = (bf16[2,18,1,512]{3,2,1,0:T(2,128)(2,1)S(1)}, bf16[2,18,1,512]{3,2,1,0:T(2,128)(2,1)S(1)}, u32[]{:S(2)}, u32[]{:S(2)}) collective-permute-start(bf16[2,18,1,512]{3,2,1,0:T(2,128)(2,1)S(1)} %get-tuple-element.182), channel_id=1, source_target_pairs={{0,1},{1,2},{2,3},{4,5},{5,6},{6,7},{8,9},{9,10},{10,11},{12,13},{... | collective-permute-start | bytes 110600 | tf_op jit(solution)/shard_map/ppermute | solution.py:27
  46.8 24.2 %collective-permute-start.4 = (bf16[2,18,18,512]{3,2,1,0:T(8,128)(2,1)S(1)}, bf16[2,18,18,512]{3,2,1,0:T(8,128)(2,1)S(1)}, u32[]{:S(2)}, u32[]{:S(2)}) collective-permute-start(bf16[2,18,18,512]{3,2,1,0:T(8,128)(2,1)S(1)} %pad_maximum_fusion.10), channel_id=1, source_target_pairs={{0,8},{8,16},{16,24},{1,9},{9,17},{17,25},{2,10},{10,18},{18,26},{... | collective-permute-start | bytes 1990664 | tf_op jit(solution)/shard_map/ppermute | solution.py:38
  51.0 1.1 copy-start.3
  51.6 1.2 copy-start.2
  73.1 1.1 copy-start.1
  74.8 1.1 copy-start
  75.1 1.4 copy-start.7
  77.1 1.1 copy-start.6
  77.2 1.6 %copy-start.5 = (bf16[1,1,3,512,256]{4,3,2,1,0:T(8,128)(2,1)S(1)}, bf16[1,1,3,512,256]{4,3,2,1,0:T(8,128)(2,1)}, u32[]{:S(2)}) copy-start(bf16[1,1,3,512,256]{4,3,2,1,0:T(8,128)(2,1)} %get-tuple-element.114) | copy-start | bytes 2359300
  79.4 1.1 copy-start.4
  80.5 0.7 copy-start.32
  81.2 0.9 copy-start.30
  81.2 1.0 copy-start.31
  88.1 1.8 %copy-start.26 = (bf16[256,256]{1,0:T(8,128)(2,1)S(1)}, bf16[256,256]{1,0:T(8,128)(2,1)}, u32[]{:S(2)}) copy-start(bf16[256,256]{1,0:T(8,128)(2,1)} %get-tuple-element.127) | copy-start | bytes 393220
  88.1 1.8 %copy-start.27 = (bf16[256,256]{1,0:T(8,128)(2,1)S(1)}, bf16[256,256]{1,0:T(8,128)(2,1)}, u32[]{:S(2)}) copy-start(bf16[256,256]{1,0:T(8,128)(2,1)} %get-tuple-element.128) | copy-start | bytes 393220
  88.2 1.7 %copy-start.28 = (bf16[256,256]{1,0:T(8,128)(2,1)S(1)}, bf16[256,256]{1,0:T(8,128)(2,1)}, u32[]{:S(2)}) copy-start(bf16[256,256]{1,0:T(8,128)(2,1)} %get-tuple-element.129) | copy-start | bytes 393220
  88.2 1.7 %copy-start.29 = (bf16[256,256]{1,0:T(8,128)(2,1)S(1)}, bf16[256,256]{1,0:T(8,128)(2,1)}, u32[]{:S(2)}) copy-start(bf16[256,256]{1,0:T(8,128)(2,1)} %get-tuple-element.130) | copy-start | bytes 393220
  96.7 2.5 %copy-start.22 = (bf16[256,256]{1,0:T(8,128)(2,1)S(1)}, bf16[256,256]{1,0:T(8,128)(2,1)}, u32[]{:S(2)}) copy-start(bf16[256,256]{1,0:T(8,128)(2,1)} %get-tuple-element.131) | copy-start | bytes 393220
  96.7 2.5 %copy-start.23 = (bf16[256,256]{1,0:T(8,128)(2,1)S(1)}, bf16[256,256]{1,0:T(8,128)(2,1)}, u32[]{:S(2)}) copy-start(bf16[256,256]{1,0:T(8,128)(2,1)} %get-tuple-element.132) | copy-start | bytes 393220
  96.7 2.5 %copy-start.24 = (bf16[256,256]{1,0:T(8,128)(2,1)S(1)}, bf16[256,256]{1,0:T(8,128)(2,1)}, u32[]{:S(2)}) copy-start(bf16[256,256]{1,0:T(8,128)(2,1)} %get-tuple-element.133) | copy-start | bytes 393220
  96.7 2.5 %copy-start.25 = (bf16[256,256]{1,0:T(8,128)(2,1)S(1)}, bf16[256,256]{1,0:T(8,128)(2,1)}, u32[]{:S(2)}) copy-start(bf16[256,256]{1,0:T(8,128)(2,1)} %get-tuple-element.134) | copy-start | bytes 393220
  106.0 2.5 %copy-start.19 = (bf16[256,256]{1,0:T(8,128)(2,1)S(1)}, bf16[256,256]{1,0:T(8,128)(2,1)}, u32[]{:S(2)}) copy-start(bf16[256,256]{1,0:T(8,128)(2,1)} %get-tuple-element.135) | copy-start | bytes 393220
  106.0 2.5 %copy-start.20 = (bf16[256,256]{1,0:T(8,128)(2,1)S(1)}, bf16[256,256]{1,0:T(8,128)(2,1)}, u32[]{:S(2)}) copy-start(bf16[256,256]{1,0:T(8,128)(2,1)} %get-tuple-element.136) | copy-start | bytes 393220
  106.0 2.5 %copy-start.21 = (bf16[256,256]{1,0:T(8,128)(2,1)S(1)}, bf16[256,256]{1,0:T(8,128)(2,1)}, u32[]{:S(2)}) copy-start(bf16[256,256]{1,0:T(8,128)(2,1)} %get-tuple-element.137) | copy-start | bytes 393220
  116.9 1.0 copy-start.9
  116.9 1.2 copy-start.10
  117.0 1.4 copy-start.11
  117.0 1.4 copy-start.12
  117.0 1.6 %copy-start.13 = (f32[2,16,16,1,256]{4,2,1,0,3:T(8,128)S(1)}, f32[2,16,16,1,256]{4,2,1,0,3:T(8,128)}, u32[]{:S(2)}) copy-start(f32[2,16,16,1,256]{4,2,1,0,3:T(8,128)} %copy.86) | copy-start | bytes 1572868
  117.0 1.7 %copy-start.14 = (f32[2,16,16,1,256]{4,2,1,0,3:T(8,128)S(1)}, f32[2,16,16,1,256]{4,2,1,0,3:T(8,128)}, u32[]{:S(2)}) copy-start(f32[2,16,16,1,256]{4,2,1,0,3:T(8,128)} %copy.87) | copy-start | bytes 1572868
  119.0 1.0 copy-start.15
  119.1 1.2 copy-start.16
  119.1 1.3 copy-start.17
  119.1 1.5 %copy-start.18 = (f32[2,16,16,1,256]{4,2,1,0,3:T(8,128)S(1)}, f32[2,16,16,1,256]{4,2,1,0,3:T(8,128)}, u32[]{:S(2)}) copy-start(f32[2,16,16,1,256]{4,2,1,0,3:T(8,128)} %copy.91) | copy-start | bytes 1572868
  123.7 3.4 %collective-permute-start.5 = (bf16[2,34,256]{2,0,1:T(2,128)(2,1)S(1)}, bf16[2,34,256]{2,0,1:T(2,128)(2,1)S(1)}, u32[]{:S(2)}, u32[]{:S(2)}) collective-permute-start(bf16[2,34,256]{2,0,1:T(2,128)(2,1)S(1)} %get-tuple-element.162), channel_id=1, source_target_pairs={{0,4},{1,5},{2,6},{3,7},{8,12},{9,13},{10,14},{11,15},{16,20},{17,... | collective-permute-start | bytes 104456 | tf_op jit(solution)/shard_map/ppermute | solution.py:38
  125.8 4.7 %collective-permute-start.6 = (bf16[2,34,256]{2,0,1:T(2,128)(2,1)S(1)}, bf16[2,34,256]{2,0,1:T(2,128)(2,1)S(1)}, u32[]{:S(2)}, u32[]{:S(2)}) collective-permute-start(bf16[2,34,256]{2,0,1:T(2,128)(2,1)S(1)} %get-tuple-element.161), channel_id=1, source_target_pairs={{4,0},{5,1},{6,2},{7,3},{12,8},{13,9},{14,10},{15,11},{20,16},{21,... | collective-permute-start | bytes 104456 | tf_op jit(solution)/shard_map/ppermute | solution.py:38
  133.7 7.6 %copy-start.33 = (f32[256]{0:T(256)S(1)}, f32[256]{0:T(256)}, u32[]{:S(2)}) copy-start(f32[256]{0:T(256)} %param.23) | copy-start | bytes 3076
  133.7 5.3 %collective-permute-start.7 = (bf16[2,32,256]{2,1,0:T(8,128)(2,1)S(1)}, bf16[2,32,256]{2,1,0:T(8,128)(2,1)S(1)}, u32[]{:S(2)}, u32[]{:S(2)}) collective-permute-start(bf16[2,32,256]{2,1,0:T(8,128)(2,1)S(1)} %get-tuple-element.164), channel_id=1, source_target_pairs={{0,1},{1,2},{2,3},{4,5},{5,6},{6,7},{8,9},{9,10},{10,11},{12,13},{... | collective-permute-start | bytes 98312 | tf_op jit(solution)/shard_map/ppermute | solution.py:38
  136.0 5.2 %collective-permute-start.8 = (bf16[2,32,256]{2,1,0:T(8,128)(2,1)S(1)}, bf16[2,32,256]{2,1,0:T(8,128)(2,1)S(1)}, u32[]{:S(2)}, u32[]{:S(2)}) collective-permute-start(bf16[2,32,256]{2,1,0:T(8,128)(2,1)S(1)} %get-tuple-element.163), channel_id=1, source_target_pairs={{1,0},{2,1},{3,2},{5,4},{6,5},{7,6},{9,8},{10,9},{11,10},{13,12},{... | collective-permute-start | bytes 98312 | tf_op jit(solution)/shard_map/ppermute | solution.py:38
where the time goes:
time: 144 us; the launch traced here: 143 us
  local copies, waits for them, and re-layouts  54.6 us (38%)
  starting transfers between devices  25.2 us (18%)
  waiting for transfers between devices  22.9 us (16%)
  blocking collectives  18.8 us (13%)
  matrix products  10.9 us (8%)
  other arithmetic  9.36 us (6%)
    ppermute x5, waiting for transfers between devices, from_behind(): return lax.ppermute(array, axis, pairs)  22.7 us
    unnamed x89, local copies, waits for them, and re-layouts  17.8 us
    psum x1, blocking collectives, shards(): lax.psum((tile_sums, tile_squares), ('ha', 'wa'))  11.8 us
    slice x4, local copies, waits for them, and re-layouts, upsample_tile(): product[:, :, :, 2 * shift_row + shift_col]  11.6 us
    ppermute x5, starting transfers between devices, from_behind(): return lax.ppermute(array, axis, pairs)  11 us
    reshape x4, local copies, waits for them, and re-layouts, upsample_tile(): jnp.dot(flat, joined, preferred_element_type=jnp.float32)  8.62 us
    ppermute x2, starting transfers between devices, padded_2(): lax.ppermute(lax.slice_in_dim(block, 0, width, axis=dim), axis, backward)  8.3 us
    unnamed x1, blocking collectives  6.94 us
  transfers between devices with their start and end apart: 9, of which 4 were waited for; matrix products, arithmetic and copies ran while one was open for 8% of the time, Pallas kernels for 0%

commit v1 on v0

--- a/solution.py
+++ b/solution.py
@@ -104,7 +104,7 @@
     frames, height, breadth, channels = latent.shape
     block_index = lax.axis_index("tm")
     tile_sums, tile_squares = group_totals(latent)
-    block_sums, block_squares = lax.psum((tile_sums, tile_squares), ("ha", "wa"))
+    block_sums, block_squares = lax.psum(lax.psum((tile_sums, tile_squares), "wa"), "ha")
     zeros_pair = (jnp.zeros_like(block_sums), jnp.zeros_like(block_squares))
     before = prefix((block_sums, block_squares), "tm", add_pair, zeros_pair)
     upto_sums = before[0] + block_sums

time: 144 us -> 144 us (level)
  blocking collectives: 18.8 us -> 16.4 us
    psum x1 -> x2, blocking collectives: 11.8 us -> 9.47 us  [the longest x1 5.69 us: shards(): lax.psum((tile_sums, tile_squares), 'wa')]
where the time goes in v1:
time: 144 us; the launch traced here: 143 us
  local copies, waits for them, and re-layouts  54.6 us (38%)
  starting transfers between devices  26.2 us (18%)
  waiting for transfers between devices  24.1 us (17%)
  blocking collectives  16.4 us (11%)
  matrix products  10.9 us (8%)
  other arithmetic  9.36 us (6%)
    ppermute x5, waiting for transfers between devices, from_behind(): return lax.ppermute(array, axis, pairs)  23.9 us
    unnamed x89, local copies, waits for them, and re-layouts  17.8 us
    slice x4, local copies, waits for them, and re-layouts, upsample_tile(): product[:, :, :, 2 * shift_row + shift_col]  11.7 us
    ppermute x5, starting transfers between devices, from_behind(): return lax.ppermute(array, axis, pairs)  11.4 us
    ppermute x2, starting transfers between devices, padded_2(): lax.ppermute(lax.slice_in_dim(block, 0, width, axis=dim), axis, backward)  8.81 us
    reshape x4, local copies, waits for them, and re-layouts, upsample_tile(): jnp.dot(flat, joined, preferred_element_type=jnp.float32)  8.6 us
    unnamed x1, blocking collectives  6.94 us
    ppermute x2, starting transfers between devices, padded_2(): lax.ppermute(lax.slice_in_dim(block, block.shape[dim] - width, None, axis...  6.01 us
  transfers between devices with their start and end apart: 9, of which 4 were waited for; matrix products, arithmetic and copies ran while one was open for 8% of the time, Pallas kernels for 0%

profile of v1, /device:TPU:9, one launch (start us, length us, event | category | flops | bytes accessed | tf_op | source)
XLA Modules:
  0.0 142.9 jit_solution(8139991736967778958)
XLA Ops:
  0.0 1.2 fusion.9
  1.6 5.7 %all-reduce.18 = (f32[32]{0:T(128)S(1)}, f32[32]{0:T(128)S(1)}) all-reduce(f32[32]{0:T(128)S(1)} %reduce_sum.37, f32[32]{0:T(128)S(1)} %reduce_sum.39), channel_id=1, replica_groups=mesh['tm'=4,'ha'=2,'wa'=4] {'wa'}, use_global_device_ids=true, to_apply=%region_2.0 | all-reduce | flops 64 | bytes 512 | tf_op jit(solution)/shard_map/psum | solution.py:107
  7.3 3.8 %all-reduce.20 = (f32[32]{0:T(128)S(1)}, f32[32]{0:T(128)S(1)}) all-reduce(f32[32]{0:T(128)S(1)} %get-tuple-element.103, f32[32]{0:T(128)S(1)} %get-tuple-element.104), channel_id=1, replica_groups=mesh['tm'=4,'ha'=2,'wa'=4] {'ha'}, use_global_device_ids=true, to_apply=%region_3.0 | all-reduce | flops 64 | bytes 512 | tf_op jit(solution)/shard_map/psum | solution.py:107
  11.1 1.2 dynamic-slice.32
  13.3 6.9 %all-reduce.19 = (f32[128]{0:T(128)S(1)}, f32[128]{0:T(128)S(1)}) all-reduce(f32[128]{0:T(128)S(1)} %dynamic-update-slice.12, f32[128]{0:T(128)S(1)} %dynamic-update-slice.13), channel_id=2, replica_groups=mesh['tm'=4,'ha'=2,'wa'=4] {'tm'}, use_global_device_ids=true, to_apply=%add.16 | all-reduce | flops 256 | bytes 2048
  20.8 1.4 %fusion.18 = bf16[2,16,16,512]{3,2,1,0:T(8,128)(2,1)S(1)} fusion(bf16[2,16,16,512]{3,2,1,0:T(8,128)(2,1)} %param.17, f32[512]{0:T(512)} %param.19, f32[512]{0:T(512)} %param.18, f32[512]{0:T(512)S(1)} %mul.34, f32[512]{0:T(512)S(1)} %sub.13), kind=kLoop, calls=%fused_computation.42 | loop fusion | flops 2621440 | bytes 1056768 | tf_op jit(solution)/shard_map/convert_element_type | solution.py:124
  22.2 1.3 collective-permute-start.1
  23.5 4.0 %collective-permute-start = (bf16[2,1,16,512]{3,2,1,0:T(8,128)(2,1)S(1)}, bf16[2,1,16,512]{3,2,1,0:T(8,128)(2,1)S(1)}, u32[]{:S(2)}, u32[]{:S(2)}) collective-permute-start(bf16[2,1,16,512]{3,2,1,0:T(8,128)(2,1)S(1)} %get-tuple-element.189), channel_id=1, source_target_pairs={{0,4},{1,5},{2,6},{3,7},{8,12},{9,13},{10,14},{11,15},{16,20},{17,... | collective-permute-start | bytes 98312 | tf_op jit(solution)/shard_map/ppermute | solution.py:27
  27.5 5.9 %fusion.58 = (bf16[1,1,3,512,256]{4,3,2,1,0:T(8,128)(2,1)S(1)}, bf16[1,1,3,512,256]{4,3,2,1,0:T(8,128)(2,1)}, bf16[1,1,3,512,256]{4,3,2,1,0:T(8,128)(2,1)}, bf16...) fusion(bf16[3,3,3,512,256]{4,3,2,1,0:T(8,128)(2,1)} %param.20), kind=kLoop, calls=%fused_computation.136 | loop fusion | bytes 14155776 | tf_op jit(solution)/shard_map/slice | solution.py:66
  33.6 7.5 %collective-permute-start.3 = (bf16[2,18,1,512]{3,2,1,0:T(2,128)(2,1)S(1)}, bf16[2,18,1,512]{3,2,1,0:T(2,128)(2,1)S(1)}, u32[]{:S(2)}, u32[]{:S(2)}) collective-permute-start(bf16[2,18,1,512]{3,2,1,0:T(2,128)(2,1)S(1)} %get-tuple-element.185), channel_id=1, source_target_pairs={{1,0},{2,1},{3,2},{5,4},{6,5},{7,6},{9,8},{10,9},{11,10},{13,12},{... | collective-permute-start | bytes 110600 | tf_op jit(solution)/shard_map/ppermute | solution.py:30
  41.1 2.0 %collective-permute-start.2 = (bf16[2,18,1,512]{3,2,1,0:T(2,128)(2,1)S(1)}, bf16[2,18,1,512]{3,2,1,0:T(2,128)(2,1)S(1)}, u32[]{:S(2)}, u32[]{:S(2)}) collective-permute-start(bf16[2,18,1,512]{3,2,1,0:T(2,128)(2,1)S(1)} %get-tuple-element.184), channel_id=1, source_target_pairs={{0,1},{1,2},{2,3},{4,5},{5,6},{6,7},{8,9},{9,10},{10,11},{12,13},{... | collective-permute-start | bytes 110600 | tf_op jit(solution)/shard_map/ppermute | solution.py:27
  43.2 1.2 slice_bitcast_fusion.15
  45.1 3.2 %collective-permute-start.4 = (bf16[2,18,18,512]{3,2,1,0:T(8,128)(2,1)S(1)}, bf16[2,18,18,512]{3,2,1,0:T(8,128)(2,1)S(1)}, u32[]{:S(2)}, u32[]{:S(2)}) collective-permute-start(bf16[2,18,18,512]{3,2,1,0:T(8,128)(2,1)S(1)} %pad_maximum_fusion.10), channel_id=1, source_target_pairs={{0,8},{8,16},{16,24},{1,9},{9,17},{17,25},{2,10},{10,18},{18,26},{... | collective-permute-start | bytes 1990664 | tf_op jit(solution)/shard_map/ppermute | solution.py:38
  51.6 17.7 %collective-permute-done.4 = bf16[2,18,18,512]{3,2,1,0:T(8,128)(2,1)S(1)} collective-permute-done((bf16[2,18,18,512]{3,2,1,0:T(8,128)(2,1)S(1)}, bf16[2,18,18,512]{3,2,1,0:T(8,128)(2,1)S(1)}, u32[]{:S(2)}, u32[]{:S(2)}) %collective-permute-start.4) | collective-permute-done | bytes 663584 | tf_op jit(solution)/shard_map/ppermute | solution.py:38
  71.7 0.8 copy-done.1
  75.6 1.0 copy-done.6
  77.8 1.0 copy-done.4
  80.5 1.8 %fusion.43 = f32[512,1024]{1,0:T(8,128)} fusion(bf16[512,256]{1,0:T(8,128)(2,1)S(1)} %fusion.8, bf16[256,256]{1,0:T(8,128)(2,1)S(1)} %copy-done.30, bf16[256,256]{1,0:T(8,128)(2,1)S(1)} %copy-done.31, bf16[256,256]{1,0:T(8,128)(2,1)S(1)} %get-tuple-element.127, bf16[256,256]{1,0:T(8,128)(2,1)S(1)} %get-tuple-element.128), kind=kOutput, calls=%fused_computation.75 | convolution fusion | flops 270532608 | bytes 2883584 | tf_op jit(solution)/shard_map/dot_general | solution.py:88
  82.3 2.2 %reshape.235 = f32[2,16,16,4,256]{4,3,2,1,0:T(4,128)S(1)} reshape(f32[512,1024]{1,0:T(8,128)} %fusion.43) | data formatting | bytes 4194304 | tf_op jit(solution)/shard_map/reshape | solution.py:88
  84.5 1.9 %fusion.62 = (f32[2,16,16,1,256]{4,3,2,1,0:T(1,128)S(1)}, f32[2,16,16,1,256]{4,3,2,1,0:T(1,128)S(1)}, f32[2,16,16,1,256]{4,3,2,1,0:T(1,128)S(1)}, f32[2,16,16,1,256]{4,3,2,1,0:T(1,128)S(1)}) fusion(f32[2,16,16,4,256]{4,3,2,1,0:T(4,128)S(1)} %reshape.235), kind=kLoop, calls=%fused_computation.140 | loop fusion | bytes 4194304 | tf_op jit(solution)/shard_map/slice | solution.py:95
  86.6 0.8 copy.82
  87.4 0.8 copy.83
  88.2 1.8 %fusion.35 = f32[512,1024]{1,0:T(8,128)} fusion(bf16[512,256]{1,0:T(8,128)(2,1)S(1)} %fusion.8, bf16[256,256]{1,0:T(8,128)(2,1)S(1)} %copy-done.26, bf16[256,256]{1,0:T(8,128)(2,1)S(1)} %copy-done.27, bf16[256,256]{1,0:T(8,128)(2,1)S(1)} %copy-done.28, bf16[256,256]{1,0:T(8,128)(2,1)S(1)} %copy-done.29), kind=kOutput, calls=%fused_computation.67 | convolution fusion | flops 270532608 | bytes 2883584 | tf_op jit(solution)/shard_map/dot_general | solution.py:88
  90.0 2.2 %reshape.234 = f32[2,16,16,4,256]{4,3,2,1,0:T(4,128)S(1)} reshape(f32[512,1024]{1,0:T(8,128)} %fusion.35) | data formatting | bytes 4194304 | tf_op jit(solution)/shard_map/reshape | solution.py:88
  92.2 1.9 %fusion.61 = (f32[2,16,16,1,256]{4,3,2,1,0:T(1,128)S(1)}, f32[2,16,16,1,256]{4,3,2,1,0:T(1,128)S(1)}, f32[2,16,16,1,256]{4,3,2,1,0:T(1,128)S(1)}, f32[2,16,16,1,256]{4,3,2,1,0:T(1,128)S(1)}) fusion(f32[2,16,16,4,256]{4,3,2,1,0:T(4,128)S(1)} %reshape.234), kind=kLoop, calls=%fused_computation.139 | loop fusion | bytes 4194304 | tf_op jit(solution)/shard_map/slice | solution.py:95
  94.2 0.8 copy.84
  95.8 0.8 copy.86
  96.7 0.8 copy.87
  97.5 1.8 %fusion.27 = f32[512,1024]{1,0:T(8,128)} fusion(bf16[512,256]{1,0:T(8,128)(2,1)S(1)} %fusion.8, bf16[256,256]{1,0:T(8,128)(2,1)S(1)} %copy-done.22, bf16[256,256]{1,0:T(8,128)(2,1)S(1)} %copy-done.23, bf16[256,256]{1,0:T(8,128)(2,1)S(1)} %copy-done.24, bf16[256,256]{1,0:T(8,128)(2,1)S(1)} %copy-done.25), kind=kOutput, calls=%fused_computation.59 | convolution fusion | flops 270532608 | bytes 2883584 | tf_op jit(solution)/shard_map/dot_general | solution.py:88
  99.3 2.2 %reshape.233 = f32[2,16,16,4,256]{4,3,2,1,0:T(4,128)S(1)} reshape(f32[512,1024]{1,0:T(8,128)} %fusion.27) | data formatting | bytes 4194304 | tf_op jit(solution)/shard_map/reshape | solution.py:88
  101.5 1.9 %fusion.60 = (f32[2,16,16,1,256]{4,3,2,1,0:T(1,128)S(1)}, f32[2,16,16,1,256]{4,3,2,1,0:T(1,128)S(1)}, f32[2,16,16,1,256]{4,3,2,1,0:T(1,128)S(1)}, f32[2,16,16,1,256]{4,3,2,1,0:T(1,128)S(1)}) fusion(f32[2,16,16,4,256]{4,3,2,1,0:T(4,128)S(1)} %reshape.233), kind=kLoop, calls=%fused_computation.138 | loop fusion | bytes 4194304 | tf_op jit(solution)/shard_map/slice | solution.py:95
  103.5 0.9 copy.88
  104.3 0.8 copy.89
  105.2 0.8 copy.90
  106.0 0.8 copy.91
  107.3 2.0 %reshape.232 = f32[2,16,16,4,256]{4,3,2,1,0:T(4,128)} reshape(f32[512,1024]{1,0:T(8,128)S(1)} %fusion.19) | data formatting | bytes 4194304 | tf_op jit(solution)/shard_map/reshape | solution.py:88
  109.3 5.9 %fusion.59 = (f32[2,16,16,1,256]{4,3,2,1,0:T(1,128)S(1)}, f32[2,16,16,1,256]{4,3,2,1,0:T(1,128)S(1)}, f32[2,16,16,1,256]{4,3,2,1,0:T(1,128)S(1)}, f32[2,16,16,1,256]{4,3,2,1,0:T(1,128)S(1)}) fusion(f32[2,16,16,4,256]{4,3,2,1,0:T(4,128)} %reshape.232), kind=kLoop, calls=%fused_computation.137 | loop fusion | bytes 4194304 | tf_op jit(solution)/shard_map/slice | solution.py:95
  115.4 0.9 copy-done.9
  117.6 0.9 copy-done.15
  120.0 1.2 copy.43
  122.1 1.3 collective-permute-start.5
  124.2 1.3 collective-permute-start.6
  126.0 2.9 %collective-permute-done.6 = bf16[2,34,256]{2,0,1:T(2,128)(2,1)S(1)} collective-permute-done((bf16[2,34,256]{2,0,1:T(2,128)(2,1)S(1)}, bf16[2,34,256]{2,0,1:T(2,128)(2,1)S(1)}, u32[]{:S(2)}, u32[]{:S(2)}) %collective-permute-start.6) | collective-permute-done | bytes 34848 | tf_op jit(solution)/shard_map/ppermute | solution.py:38
  129.0 2.8 %scatter-add.15 = f32[2,32,34,256]{3,1,0,2:T(8,128)S(1)} dynamic-update-slice(f32[2,32,34,256]{3,1,0,2:T(8,128)S(1)} %copy.45, f32[2,1,34,256]{3,1,0,2:T(1,128)S(1)} %copy_add_fusion, s32[]{:T(128)} %constant.128.clone.1, s32[]{:T(128)} %constant.134.clone.1, s32[]{:T(128)} %constant.128.clone.1, s32[]{:T(128)} %constant.128.clone.1) | dynamic-update-slice | bytes 139268 | tf_op jit(solution)/shard_map/scatter-add | solution.py:142
  132.0 3.6 %collective-permute-start.7 = (bf16[2,32,256]{2,1,0:T(8,128)(2,1)S(1)}, bf16[2,32,256]{2,1,0:T(8,128)(2,1)S(1)}, u32[]{:S(2)}, u32[]{:S(2)}) collective-permute-start(bf16[2,32,256]{2,1,0:T(8,128)(2,1)S(1)} %get-tuple-element.166), channel_id=1, source_target_pairs={{0,1},{1,2},{2,3},{4,5},{5,6},{6,7},{8,9},{9,10},{10,11},{12,13},{... | collective-permute-start | bytes 98312 | tf_op jit(solution)/shard_map/ppermute | solution.py:38
  135.8 1.9 %collective-permute-start.8 = (bf16[2,32,256]{2,1,0:T(8,128)(2,1)S(1)}, bf16[2,32,256]{2,1,0:T(8,128)(2,1)S(1)}, u32[]{:S(2)}, u32[]{:S(2)}) collective-permute-start(bf16[2,32,256]{2,1,0:T(8,128)(2,1)S(1)} %get-tuple-element.165), channel_id=1, source_target_pairs={{1,0},{2,1},{3,2},{5,4},{6,5},{7,6},{9,8},{10,9},{11,10},{13,12},{... | collective-permute-start | bytes 98312 | tf_op jit(solution)/shard_map/ppermute | solution.py:38
  137.8 3.3 %collective-permute-done.8 = bf16[2,32,256]{2,1,0:T(8,128)(2,1)S(1)} collective-permute-done((bf16[2,32,256]{2,1,0:T(8,128)(2,1)S(1)}, bf16[2,32,256]{2,1,0:T(8,128)(2,1)S(1)}, u32[]{:S(2)}, u32[]{:S(2)}) %collective-permute-start.8) | collective-permute-done | bytes 32800 | tf_op jit(solution)/shard_map/ppermute | solution.py:38
  141.4 1.6 %copy.46 = bf16[2,32,32,256]{3,2,1,0:T(8,128)(2,1)} copy(bf16[2,32,32,256]{3,1,0,2:T(8,128)(2,1)S(1)} %add_convert_fusion) | data formatting | bytes 2097152 | tf_op jit(solution)/shard_map/convert_element_type | solution.py:148
  (141 shorter events, 20.7 us)
Async XLA Ops:
  22.2 11.2 %collective-permute-start.1 = (bf16[2,1,16,512]{3,2,1,0:T(8,128)(2,1)S(1)}, bf16[2,1,16,512]{3,2,1,0:T(8,128)(2,1)S(1)}, u32[]{:S(2)}, u32[]{:S(2)}) collective-permute-start(bf16[2,1,16,512]{3,2,1,0:T(8,128)(2,1)S(1)} %get-tuple-element.190), channel_id=1, source_target_pairs={{4,0},{5,1},{6,2},{7,3},{12,8},{13,9},{14,10},{15,11},{20,16},{21,... | collective-permute-start | bytes 98312 | tf_op jit(solution)/shard_map/ppermute | solution.py:30
  23.5 9.9 %collective-permute-start = (bf16[2,1,16,512]{3,2,1,0:T(8,128)(2,1)S(1)}, bf16[2,1,16,512]{3,2,1,0:T(8,128)(2,1)S(1)}, u32[]{:S(2)}, u32[]{:S(2)}) collective-permute-start(bf16[2,1,16,512]{3,2,1,0:T(8,128)(2,1)S(1)} %get-tuple-element.189), channel_id=1, source_target_pairs={{0,4},{1,5},{2,6},{3,7},{8,12},{9,13},{10,14},{11,15},{16,20},{17,... | collective-permute-start | bytes 98312 | tf_op jit(solution)/shard_map/ppermute | solution.py:27
  27.5 15.6 %copy-start.8 = (bf16[4,4,256,256]{3,2,1,0:T(8,128)(2,1)S(1)}, bf16[4,4,256,256]{3,2,1,0:T(8,128)(2,1)}, u32[]{:S(2)}) copy-start(bf16[4,4,256,256]{3,2,1,0:T(8,128)(2,1)} %param.22) | copy-start | bytes 6291460
  33.6 10.8 %collective-permute-start.3 = (bf16[2,18,1,512]{3,2,1,0:T(2,128)(2,1)S(1)}, bf16[2,18,1,512]{3,2,1,0:T(2,128)(2,1)S(1)}, u32[]{:S(2)}, u32[]{:S(2)}) collective-permute-start(bf16[2,18,1,512]{3,2,1,0:T(2,128)(2,1)S(1)} %get-tuple-element.185), channel_id=1, source_target_pairs={{1,0},{2,1},{3,2},{5,4},{6,5},{7,6},{9,8},{10,9},{11,10},{13,12},{... | collective-permute-start | bytes 110600 | tf_op jit(solution)/shard_map/ppermute | solution.py:30
  41.1 3.4 %collective-permute-start.2 = (bf16[2,18,1,512]{3,2,1,0:T(2,128)(2,1)S(1)}, bf16[2,18,1,512]{3,2,1,0:T(2,128)(2,1)S(1)}, u32[]{:S(2)}, u32[]{:S(2)}) collective-permute-start(bf16[2,18,1,512]{3,2,1,0:T(2,128)(2,1)S(1)} %get-tuple-element.184), channel_id=1, source_target_pairs={{0,1},{1,2},{2,3},{4,5},{5,6},{6,7},{8,9},{9,10},{10,11},{12,13},{... | collective-permute-start | bytes 110600 | tf_op jit(solution)/shard_map/ppermute | solution.py:27
  45.1 24.3 %collective-permute-start.4 = (bf16[2,18,18,512]{3,2,1,0:T(8,128)(2,1)S(1)}, bf16[2,18,18,512]{3,2,1,0:T(8,128)(2,1)S(1)}, u32[]{:S(2)}, u32[]{:S(2)}) collective-permute-start(bf16[2,18,18,512]{3,2,1,0:T(8,128)(2,1)S(1)} %pad_maximum_fusion.10), channel_id=1, source_target_pairs={{0,8},{8,16},{16,24},{1,9},{9,17},{17,25},{2,10},{10,18},{18,26},{... | collective-permute-start | bytes 1990664 | tf_op jit(solution)/shard_map/ppermute | solution.py:38
  49.3 1.1 copy-start.3
  49.8 1.2 copy-start.2
  71.4 1.1 copy-start.1
  73.1 1.1 copy-start
  73.4 1.4 copy-start.7
  75.4 1.1 copy-start.6
  75.5 1.6 %copy-start.5 = (bf16[1,1,3,512,256]{4,3,2,1,0:T(8,128)(2,1)S(1)}, bf16[1,1,3,512,256]{4,3,2,1,0:T(8,128)(2,1)}, u32[]{:S(2)}) copy-start(bf16[1,1,3,512,256]{4,3,2,1,0:T(8,128)(2,1)} %get-tuple-element.116) | copy-start | bytes 2359300
  77.7 1.1 copy-start.4
  78.9 0.7 copy-start.32
  79.5 0.9 copy-start.30
  79.5 1.0 copy-start.31
  86.5 1.8 %copy-start.26 = (bf16[256,256]{1,0:T(8,128)(2,1)S(1)}, bf16[256,256]{1,0:T(8,128)(2,1)}, u32[]{:S(2)}) copy-start(bf16[256,256]{1,0:T(8,128)(2,1)} %get-tuple-element.129) | copy-start | bytes 393220
  86.5 1.7 %copy-start.27 = (bf16[256,256]{1,0:T(8,128)(2,1)S(1)}, bf16[256,256]{1,0:T(8,128)(2,1)}, u32[]{:S(2)}) copy-start(bf16[256,256]{1,0:T(8,128)(2,1)} %get-tuple-element.130) | copy-start | bytes 393220
  86.5 1.7 %copy-start.28 = (bf16[256,256]{1,0:T(8,128)(2,1)S(1)}, bf16[256,256]{1,0:T(8,128)(2,1)}, u32[]{:S(2)}) copy-start(bf16[256,256]{1,0:T(8,128)(2,1)} %get-tuple-element.131) | copy-start | bytes 393220
  86.5 1.7 %copy-start.29 = (bf16[256,256]{1,0:T(8,128)(2,1)S(1)}, bf16[256,256]{1,0:T(8,128)(2,1)}, u32[]{:S(2)}) copy-start(bf16[256,256]{1,0:T(8,128)(2,1)} %get-tuple-element.132) | copy-start | bytes 393220
  95.0 2.5 %copy-start.22 = (bf16[256,256]{1,0:T(8,128)(2,1)S(1)}, bf16[256,256]{1,0:T(8,128)(2,1)}, u32[]{:S(2)}) copy-start(bf16[256,256]{1,0:T(8,128)(2,1)} %get-tuple-element.133) | copy-start | bytes 393220
  95.0 2.5 %copy-start.23 = (bf16[256,256]{1,0:T(8,128)(2,1)S(1)}, bf16[256,256]{1,0:T(8,128)(2,1)}, u32[]{:S(2)}) copy-start(bf16[256,256]{1,0:T(8,128)(2,1)} %get-tuple-element.134) | copy-start | bytes 393220
  95.0 2.5 %copy-start.24 = (bf16[256,256]{1,0:T(8,128)(2,1)S(1)}, bf16[256,256]{1,0:T(8,128)(2,1)}, u32[]{:S(2)}) copy-start(bf16[256,256]{1,0:T(8,128)(2,1)} %get-tuple-element.135) | copy-start | bytes 393220
  95.0 2.5 %copy-start.25 = (bf16[256,256]{1,0:T(8,128)(2,1)S(1)}, bf16[256,256]{1,0:T(8,128)(2,1)}, u32[]{:S(2)}) copy-start(bf16[256,256]{1,0:T(8,128)(2,1)} %get-tuple-element.136) | copy-start | bytes 393220
  104.3 2.5 %copy-start.19 = (bf16[256,256]{1,0:T(8,128)(2,1)S(1)}, bf16[256,256]{1,0:T(8,128)(2,1)}, u32[]{:S(2)}) copy-start(bf16[256,256]{1,0:T(8,128)(2,1)} %get-tuple-element.137) | copy-start | bytes 393220
  104.3 2.5 %copy-start.20 = (bf16[256,256]{1,0:T(8,128)(2,1)S(1)}, bf16[256,256]{1,0:T(8,128)(2,1)}, u32[]{:S(2)}) copy-start(bf16[256,256]{1,0:T(8,128)(2,1)} %get-tuple-element.138) | copy-start | bytes 393220
  104.3 2.5 %copy-start.21 = (bf16[256,256]{1,0:T(8,128)(2,1)S(1)}, bf16[256,256]{1,0:T(8,128)(2,1)}, u32[]{:S(2)}) copy-start(bf16[256,256]{1,0:T(8,128)(2,1)} %get-tuple-element.139) | copy-start | bytes 393220
  115.2 1.0 copy-start.9
  115.2 1.2 copy-start.10
  115.3 1.4 copy-start.11
  115.3 1.4 copy-start.12
  115.4 1.6 %copy-start.13 = (f32[2,16,16,1,256]{4,2,1,0,3:T(8,128)S(1)}, f32[2,16,16,1,256]{4,2,1,0,3:T(8,128)}, u32[]{:S(2)}) copy-start(f32[2,16,16,1,256]{4,2,1,0,3:T(8,128)} %copy.86) | copy-start | bytes 1572868
  115.4 1.7 %copy-start.14 = (f32[2,16,16,1,256]{4,2,1,0,3:T(8,128)S(1)}, f32[2,16,16,1,256]{4,2,1,0,3:T(8,128)}, u32[]{:S(2)}) copy-start(f32[2,16,16,1,256]{4,2,1,0,3:T(8,128)} %copy.87) | copy-start | bytes 1572868
  117.4 1.0 copy-start.15
  117.4 1.2 copy-start.16
  117.4 1.3 copy-start.17
  117.4 1.5 %copy-start.18 = (f32[2,16,16,1,256]{4,2,1,0,3:T(8,128)S(1)}, f32[2,16,16,1,256]{4,2,1,0,3:T(8,128)}, u32[]{:S(2)}) copy-start(f32[2,16,16,1,256]{4,2,1,0,3:T(8,128)} %copy.91) | copy-start | bytes 1572868
  122.1 3.4 %collective-permute-start.5 = (bf16[2,34,256]{2,0,1:T(2,128)(2,1)S(1)}, bf16[2,34,256]{2,0,1:T(2,128)(2,1)S(1)}, u32[]{:S(2)}, u32[]{:S(2)}) collective-permute-start(bf16[2,34,256]{2,0,1:T(2,128)(2,1)S(1)} %get-tuple-element.164), channel_id=1, source_target_pairs={{0,4},{1,5},{2,6},{3,7},{8,12},{9,13},{10,14},{11,15},{16,20},{17,... | collective-permute-start | bytes 104456 | tf_op jit(solution)/shard_map/ppermute | solution.py:38
  124.2 4.7 %collective-permute-start.6 = (bf16[2,34,256]{2,0,1:T(2,128)(2,1)S(1)}, bf16[2,34,256]{2,0,1:T(2,128)(2,1)S(1)}, u32[]{:S(2)}, u32[]{:S(2)}) collective-permute-start(bf16[2,34,256]{2,0,1:T(2,128)(2,1)S(1)} %get-tuple-element.163), channel_id=1, source_target_pairs={{4,0},{5,1},{6,2},{7,3},{12,8},{13,9},{14,10},{15,11},{20,16},{21,... | collective-permute-start | bytes 104456 | tf_op jit(solution)/shard_map/ppermute | solution.py:38
  132.0 9.0 %copy-start.33 = (f32[256]{0:T(256)S(1)}, f32[256]{0:T(256)}, u32[]{:S(2)}) copy-start(f32[256]{0:T(256)} %param.23) | copy-start | bytes 3076
  132.0 5.7 %collective-permute-start.7 = (bf16[2,32,256]{2,1,0:T(8,128)(2,1)S(1)}, bf16[2,32,256]{2,1,0:T(8,128)(2,1)S(1)}, u32[]{:S(2)}, u32[]{:S(2)}) collective-permute-start(bf16[2,32,256]{2,1,0:T(8,128)(2,1)S(1)} %get-tuple-element.166), channel_id=1, source_target_pairs={{0,1},{1,2},{2,3},{4,5},{5,6},{6,7},{8,9},{9,10},{10,11},{12,13},{... | collective-permute-start | bytes 98312 | tf_op jit(solution)/shard_map/ppermute | solution.py:38
  135.8 5.2 %collective-permute-start.8 = (bf16[2,32,256]{2,1,0:T(8,128)(2,1)S(1)}, bf16[2,32,256]{2,1,0:T(8,128)(2,1)S(1)}, u32[]{:S(2)}, u32[]{:S(2)}) collective-permute-start(bf16[2,32,256]{2,1,0:T(8,128)(2,1)S(1)} %get-tuple-element.165), channel_id=1, source_target_pairs={{1,0},{2,1},{3,2},{5,4},{6,5},{7,6},{9,8},{10,9},{11,10},{13,12},{... | collective-permute-start | bytes 98312 | tf_op jit(solution)/shard_map/ppermute | solution.py:38
